TPU v7x, 128 devices: a whole 4x4x4 slice. The times are simulated.
128 devices in a mesh: sta: 4 (over y), blk: 32 (over z, x, core).
Axes of the slice: x: 4, y: 4, z: 4, core: 2. Of those that a mesh axis runs over, the one named last changes fastest.
Arguments:
- sgt_block: bfloat16 [8, 32, 3072, 1024], P('sta', 'blk'), may hold values from -6 to 6
- weights_home: bfloat16 [16384, 512], P('blk'), may hold values from -0.25 to 0.25
- weights_strad: bfloat16 [16384, 512], P('blk'), may hold values from -0.25 to 0.25
- moment: bfloat16 [16384, 6], P('blk'), may hold values from -3 to 3
- source_time: float32 [16384, 16], P('blk'), may hold values from 0.02 to 0.5
- home_pos: int32 [16384], P('blk'), may hold values from 0 to 1023, as said below
- strad_pos: int32 [16384], P('blk'), may hold values from -1 to 1023, as said below
Outputs:
- seismograms: float32 [8, 16384, 1024], P('sta', 'blk')
Inputs may be any that keep to these rules, and one draw needn't show every extreme that they name: home_pos[e] // 32 names the home block and home_pos[e] % 32 a slot. The home and straddling positions of one device's events are all distinct, so no block receives more than 32 entries from one device; some block receives exactly 32 from every device. Either -1 or a position whose block strad_pos[e] // 32 is (home_pos[e] // 32 + 1) % 32.
All inputs are finite; a program needn't handle non-finite values.
Results may differ from a plain program's by a relative error of at most 0.004.
Values may be sent and summed in bfloat16 or wider, within the bound.
No kernel may reach another device: no remote copies, remote signals or barrier semaphores. Data moves between devices by JAX's collectives and lax.ppermute only.
A program may use at most 128 MiB of HBM per device.

v0:
```python
import jax
import jax.numpy as jnp
from jax import lax
from jax.experimental import pallas as pl
from jax.experimental.pallas import tpu as pltpu
from jax.sharding import PartitionSpec as P

LANES = 128
PARTS = 6
EXTRA = 8
VMEM = 60 * 1024 * 1024


def contract_last(left, right):
    return lax.dot_general(left, right, (((1,), (1,)), ((), ())), preferred_element_type=jnp.float32)


def pack_kernel(capacity, home_ref, strad_ref, wh_ref, ws_ref, moment_ref, out_ref):
    step = pl.program_id(0)
    dests = out_ref.shape[0]
    slots = dests * capacity
    events, points = wh_ref.shape
    ids = lax.broadcasted_iota(jnp.int32, (slots, events), 0) + step * slots
    home = (ids == home_ref[...]).astype(jnp.float32).astype(jnp.bfloat16)
    strad = (ids == strad_ref[...]).astype(jnp.float32).astype(jnp.bfloat16)
    rows = jnp.dot(home, wh_ref[...], preferred_element_type=jnp.float32)
    rows = rows + jnp.dot(strad, ws_ref[...], preferred_element_type=jnp.float32)
    rows = rows.astype(jnp.bfloat16)
    parts = points // LANES
    for j in range(parts):
        out_ref[:, j * capacity : (j + 1) * capacity, :] = rows[:, j * LANES : (j + 1) * LANES].reshape(
            dests, capacity, LANES
        )
    wide = jnp.concatenate(
        [moment_ref[...], jnp.zeros((EXTRA - PARTS, events), jnp.bfloat16)], axis=0
    )
    across = contract_last(wide, home + strad)
    for d in range(dests):
        first = d * capacity // LANES * LANES
        shift = d * capacity % LANES
        piece = across[:, first : first + LANES]
        if shift:
            piece = pltpu.roll(piece, LANES - shift, 1)
        out_ref[d, parts * capacity :, :] = piece.astype(jnp.bfloat16)


def pack(home_row, strad_row, weights_home, weights_strad, moment, blocks):
    events, points = weights_home.shape
    capacity = 2 * events // blocks
    height = capacity * (points // LANES) + EXTRA
    dests = 8
    whole = lambda i: (0, 0)
    return pl.pallas_call(
        lambda *refs: pack_kernel(capacity, *refs),
        grid=(blocks // dests,),
        in_specs=[
            pl.BlockSpec((1, events), whole),
            pl.BlockSpec((1, events), whole),
            pl.BlockSpec((events, points), whole),
            pl.BlockSpec((events, points), whole),
            pl.BlockSpec((PARTS, events), whole),
        ],
        out_specs=pl.BlockSpec((dests, height, LANES), lambda i: (i, 0, 0)),
        out_shape=jax.ShapeDtypeStruct((blocks, height, LANES), jnp.bfloat16),
        compiler_params=pltpu.CompilerParams(vmem_limit_bytes=VMEM),
        name="pack_rows",
    )(home_row, strad_row, weights_home, weights_strad, moment)


def field_kernel(capacity, rows_ref, sgt_ref, out_ref, combined):
    sources = rows_ref.shape[0]
    points = (rows_ref.shape[1] - EXTRA) // capacity * LANES

    @pl.when((pl.program_id(0) == 0) & (pl.program_id(1) == 0))
    def _():
        pick = lax.broadcasted_iota(jnp.int32, (capacity, LANES), 0) == lax.broadcasted_iota(
            jnp.int32, (capacity, LANES), 1
        )
        pick = pick.astype(jnp.float32).astype(jnp.bfloat16)
        packed = rows_ref[:, rows_ref.shape[1] - EXTRA :, :].reshape(sources * EXTRA, LANES)
        moments = contract_last(pick, packed)
        for m in range(sources):
            for j in range(points // LANES):
                weights = rows_ref[m, j * capacity : (j + 1) * capacity, :].astype(jnp.float32)
                for c in range(PARTS):
                    scale = moments[:, m * EXTRA + c : m * EXTRA + c + 1]
                    at = c * points + j * LANES
                    combined[m * capacity : (m + 1) * capacity, at : at + LANES] = (weights * scale).astype(
                        jnp.bfloat16
                    )

    value = jnp.dot(combined[...], sgt_ref[...], preferred_element_type=jnp.float32)
    out_ref[...] = value.astype(jnp.bfloat16).reshape(out_ref.shape)


def field(rows, sgt_block, capacity):
    sources, height, _ = rows.shape
    stations, _, depth, length = sgt_block.shape
    tile = 256
    tiles = length // tile
    return pl.pallas_call(
        lambda *refs: field_kernel(capacity, *refs),
        grid=(stations, tiles),
        in_specs=[
            pl.BlockSpec((sources, height, LANES), lambda s, j: (0, 0, 0)),
            pl.BlockSpec((None, None, depth, tile), lambda s, j: (s, 0, 0, j)),
        ],
        out_specs=pl.BlockSpec((sources, capacity, tile), lambda s, j: (0, 0, s * tiles + j)),
        out_shape=jax.ShapeDtypeStruct((sources, capacity, stations * length), jnp.bfloat16),
        scratch_shapes=[pltpu.VMEM((sources * capacity, depth), jnp.bfloat16)],
        compiler_params=pltpu.CompilerParams(vmem_limit_bytes=VMEM),
        name="field_matmul",
    )(rows, sgt_block)


def shifted(pieces, count, lane):
    turned = [pltpu.roll(piece, count, 1) for piece in pieces]
    before = [jnp.zeros_like(turned[0])] + turned[:-1]
    return [jnp.where(lane < count, b, t) for b, t in zip(before, turned)]


def trace_kernel(home_ref, strad_ref, time_ref, part_ref, out_ref, chooser, trace, taps_of):
    taps, events = time_ref.shape
    slots, length = trace.shape[0] * 2, trace.shape[1]
    columns = length // LANES

    @pl.when(pl.program_id(0) == 0)
    def _():
        home = jnp.transpose(jnp.broadcast_to(home_ref[...], (LANES, events)))
        strad = jnp.transpose(jnp.broadcast_to(strad_ref[...], (LANES, events)))
        taps_of[:, :taps] = jnp.transpose(time_ref[...])
        lane = lax.broadcasted_iota(jnp.int32, (events, LANES), 1)
        for k in range(slots // LANES):
            hit = (home == lane + k * LANES) | (strad == lane + k * LANES)
            chooser[:, k * LANES : (k + 1) * LANES] = hit.astype(jnp.float32).astype(jnp.bfloat16)

    parts = part_ref[...].reshape(slots, length)
    trace[...] = jnp.dot(chooser[...], parts, preferred_element_type=jnp.float32)
    lane = lax.broadcasted_iota(jnp.int32, (8, LANES), 1)

    def rows(i, carry):
        at = pl.ds(pl.multiple_of(i * 8, 8), 8)
        pieces = [trace[at, c * LANES : (c + 1) * LANES] for c in range(columns)]
        times = taps_of[at, :]
        near = [pieces] + [shifted(pieces, b, lane) for b in range(1, 4)]
        total = None
        for a in reversed(range(taps // 4)):
            if total is not None:
                total = shifted(total, 4, lane)
            for b in range(4):
                scale = jnp.broadcast_to(times[:, 4 * a + b : 4 * a + b + 1], (8, LANES))
                terms = [scale * piece for piece in near[b]]
                total = terms if total is None else [t + u for t, u in zip(total, terms)]
        for c in range(columns):
            out_ref[at, c * LANES : (c + 1) * LANES] = total[c]
        return carry

    lax.fori_loop(0, events // 8, rows, 0)


def traces(home_row, strad_row, source_time, parts, stations):
    taps, events = source_time.shape
    sources, capacity, width = parts.shape
    length = width // stations
    return pl.pallas_call(
        trace_kernel,
        grid=(stations,),
        in_specs=[
            pl.BlockSpec((1, events), lambda s: (0, 0)),
            pl.BlockSpec((1, events), lambda s: (0, 0)),
            pl.BlockSpec((taps, events), lambda s: (0, 0)),
            pl.BlockSpec((sources, capacity, length), lambda s: (0, 0, s)),
        ],
        out_specs=pl.BlockSpec((None, events, length), lambda s: (s, 0, 0)),
        out_shape=jax.ShapeDtypeStruct((stations, events, length), jnp.float32),
        scratch_shapes=[
            pltpu.VMEM((events, sources * capacity), jnp.bfloat16),
            pltpu.VMEM((events, length), jnp.float32),
            pltpu.VMEM((events, LANES), jnp.float32),
        ],
        compiler_params=pltpu.CompilerParams(vmem_limit_bytes=VMEM),
        name="trace_convolve",
    )(home_row, strad_row, source_time, parts)


def body(sgt_block, weights_home, weights_strad, moment, source_time, home_pos, strad_pos):
    events = weights_home.shape[0]
    blocks = lax.axis_size("blk")
    capacity = 2 * events // blocks
    stations = sgt_block.shape[0]
    home_row = home_pos.reshape(1, events)
    strad_row = strad_pos.reshape(1, events)
    packed = pack(home_row, strad_row, weights_home, weights_strad, moment.T, blocks)
    rows = lax.all_to_all(packed, "blk", split_axis=0, concat_axis=0, tiled=True)
    partial_value = field(rows, sgt_block, capacity)
    returned = lax.all_to_all(partial_value, "blk", split_axis=0, concat_axis=0, tiled=True)
    return traces(home_row, strad_row, source_time.T, returned, stations)


def solution(mesh):
    placed = (
        P("sta", "blk", None, None),
        P("blk", None),
        P("blk", None),
        P("blk", None),
        P("blk", None),
        P("blk"),
        P("blk"),
    )
    return jax.shard_map(
        body, mesh=mesh, in_specs=placed, out_specs=P("sta", "blk", None), check_vma=False
    )
```

profile of v0, /device:TPU:0, one launch (start us, length us, event | category | flops | bytes accessed | tf_op | source)
XLA Modules:
  0.0 155.8 jit_solution(3172243329761129066)
XLA Ops:
  0.0 4.2 %pack_rows.1 = bf16[32,136,128]{2,1,0:T(8,128)(2,1)} custom-call(s32[1,512]{1,0:T(1,128)} %bitcast.6, s32[1,512]{1,0:T(1,128)} %bitcast.8, bf16[512,512]{1,0:T(8,128)(2,1)} %refs_2_.1, bf16[512,512]{1,0:T(8,128)(2,1)} %refs_3_.1, bf16[6,512]{1,0:T(8,128)(2,1)} %bitcast.5), custom_call_target="tpu_custom_call" | custom-call | tf_op jit(solution)/shard_map/pack_rows/pallas_call | solution.py:53
  4.2 26.9 %all_to_all.10.refs_0_ = bf16[32,136,128]{2,1,0:T(8,128)(2,1)} all-to-all(bf16[32,136,128]{2,1,0:T(8,128)(2,1)} %pack_rows.1), channel_id=1, replica_groups=mesh['sta'=4,'blk'=32] {'blk'}, dimensions={0} | all-to-all | bytes 2228224 | tf_op jit(solution)/shard_map/all_to_all | solution.py:194
  31.1 18.6 %field_matmul.1 = bf16[32,32,2048]{2,1,0:T(8,128)(2,1)} custom-call(bf16[32,136,128]{2,1,0:T(8,128)(2,1)} %all_to_all.10.refs_0_, bf16[2,1,3072,1024]{3,2,1,0:T(8,128)(2,1)} %refs_1_.1), custom_call_target="tpu_custom_call" | custom-call | tf_op jit(solution)/shard_map/field_matmul/pallas_call | solution.py:101
  49.7 55.9 %all_to_all.11.part_ref = bf16[32,32,2048]{2,1,0:T(8,128)(2,1)} all-to-all(bf16[32,32,2048]{2,1,0:T(8,128)(2,1)} %field_matmul.1), channel_id=1, replica_groups=mesh['sta'=4,'blk'=32] {'blk'}, dimensions={0} | all-to-all | bytes 8388608 | tf_op jit(solution)/shard_map/all_to_all | solution.py:196
  105.5 50.2 %trace_convolve.1 = f32[2,512,1024]{2,1,0:T(8,128)} custom-call(s32[1,512]{1,0:T(1,128)} %bitcast.7, s32[1,512]{1,0:T(1,128)} %bitcast.9, f32[16,512]{1,0:T(8,128)} %bitcast.4, bf16[32,32,2048]{2,1,0:T(8,128)(2,1)} %all_to_all.11.part_ref), custom_call_target="tpu_custom_call" | custom-call | tf_op jit(solution)/shard_map/trace_convolve/pallas_call | solution.py:165
where the time goes:
time: 157 us; the launch traced here: 156 us
  blocking collectives  82.8 us (53%)
  Pallas kernels  73 us (46%)
    all_to_all x1, blocking collectives, body(): lax.all_to_all(partial_value, 'blk', split_axis=0, concat_axis=0, tiled=T...  55.9 us
    pallas_call x1, Pallas kernels, traces(): pl.pallas_call(trace_kernel, grid=(stations,), in_specs=[pl.BlockSpec((1,...  50.2 us
    all_to_all x1, blocking collectives, body(): lax.all_to_all(packed, 'blk', split_axis=0, concat_axis=0, tiled=True)  26.9 us
    pallas_call x1, Pallas kernels, field(): pl.pallas_call(lambda *refs: field_kernel(capacity, *refs), grid=(station...  18.6 us
    pallas_call x1, Pallas kernels, pack(): pl.pallas_call(lambda *refs: pack_kernel(capacity, *refs), grid=(blocks /...  4.19 us

commit v1 on v0

v1 whole, which is shorter than its diff:
```python
import jax
import jax.numpy as jnp
from jax import lax
from jax.experimental import pallas as pl
from jax.experimental.pallas import tpu as pltpu
from jax.sharding import PartitionSpec as P

LANES = 128
PARTS = 6
EXTRA = 8
ROWS = 512
WIDTH = 256
AHEAD = 2
VMEM = 60 * 1024 * 1024


def contract_last(left, right):
    return lax.dot_general(left, right, (((1,), (1,)), ((), ())), preferred_element_type=jnp.float32)


def pack_kernel(capacity, home_ref, strad_ref, wh_ref, ws_ref, moment_ref, out_ref):
    step = pl.program_id(0)
    dests = out_ref.shape[0]
    slots = dests * capacity
    events, points = wh_ref.shape
    ids = lax.broadcasted_iota(jnp.int32, (slots, events), 0) + step * slots
    home = (ids == home_ref[...]).astype(jnp.float32).astype(jnp.bfloat16)
    strad = (ids == strad_ref[...]).astype(jnp.float32).astype(jnp.bfloat16)
    rows = jnp.dot(home, wh_ref[...], preferred_element_type=jnp.float32)
    rows = rows + jnp.dot(strad, ws_ref[...], preferred_element_type=jnp.float32)
    rows = rows.astype(jnp.bfloat16)
    parts = points // LANES
    for j in range(parts):
        out_ref[:, j * capacity : (j + 1) * capacity, :] = rows[:, j * LANES : (j + 1) * LANES].reshape(
            dests, capacity, LANES
        )
    wide = jnp.concatenate(
        [moment_ref[...], jnp.zeros((EXTRA - PARTS, events), jnp.bfloat16)], axis=0
    )
    across = contract_last(wide, home + strad)
    for d in range(dests):
        first = d * capacity // LANES * LANES
        shift = d * capacity % LANES
        piece = across[:, first : first + LANES]
        if shift:
            piece = pltpu.roll(piece, LANES - shift, 1)
        out_ref[d, parts * capacity :, :] = piece.astype(jnp.bfloat16)


def pack(home_row, strad_row, weights_home, weights_strad, moment, blocks):
    events, points = weights_home.shape
    capacity = 2 * events // blocks
    height = capacity * (points // LANES) + EXTRA
    dests = 16
    whole = lambda i: (0, 0)
    return pl.pallas_call(
        lambda *refs: pack_kernel(capacity, *refs),
        grid=(blocks // dests,),
        in_specs=[
            pl.BlockSpec((1, events), whole),
            pl.BlockSpec((1, events), whole),
            pl.BlockSpec((events, points), whole),
            pl.BlockSpec((events, points), whole),
            pl.BlockSpec((PARTS, events), whole),
        ],
        out_specs=pl.BlockSpec((dests, height, LANES), lambda i: (i, 0, 0)),
        out_shape=jax.ShapeDtypeStruct((blocks, height, LANES), jnp.bfloat16),
        compiler_params=pltpu.CompilerParams(vmem_limit_bytes=VMEM),
        name="pack_rows",
    )(home_row, strad_row, weights_home, weights_strad, moment)


def field_kernel(capacity, tiles, rows_ref, sgt_ref, out_ref, combined, field, value, loaded, saved):
    sources, height, _ = rows_ref.shape
    points = (height - EXTRA) // capacity * LANES
    slots = sources * capacity
    length = sgt_ref.shape[-1]

    def load(k, s, start, width):
        columns = pl.ds(start, width)
        return pltpu.make_async_copy(
            sgt_ref.at[s, 0, :, columns], field.at[s, :, columns], loaded.at[k]
        )

    def save(k, s, start, width):
        columns = pl.ds(s * length + start, width)
        return pltpu.make_async_copy(value.at[:, :, columns], out_ref.at[:, :, columns], saved.at[k])

    for k, tile in enumerate(tiles[:AHEAD]):
        load(k, *tile).start()
    pick = lax.broadcasted_iota(jnp.int32, (capacity, LANES), 0) == lax.broadcasted_iota(
        jnp.int32, (capacity, LANES), 1
    )
    pick = pick.astype(jnp.float32).astype(jnp.bfloat16)
    packed = rows_ref[:, height - EXTRA :, :].reshape(sources * EXTRA, LANES)
    moments = contract_last(pick, packed)
    for m in range(sources):
        for j in range(points // LANES):
            weights = rows_ref[m, j * capacity : (j + 1) * capacity, :].astype(jnp.float32)
            for c in range(PARTS):
                scale = moments[:, m * EXTRA + c : m * EXTRA + c + 1]
                at = c * points + j * LANES
                combined[m * capacity : (m + 1) * capacity, at : at + LANES] = (weights * scale).astype(
                    jnp.bfloat16
                )
    for k, (s, start, width) in enumerate(tiles):
        load(k, s, start, width).wait()
        if k + AHEAD < len(tiles):
            load(k + AHEAD, *tiles[k + AHEAD]).start()
        for m in range(0, slots, ROWS):
            part = jnp.dot(
                combined[m : m + ROWS, :], field[s, :, start : start + width], preferred_element_type=jnp.float32
            )
            value[m // capacity : (m + ROWS) // capacity, :, s * length + start : s * length + start + width] = (
                part.astype(jnp.bfloat16).reshape(ROWS // capacity, capacity, width)
            )
        save(k, s, start, width).start()
    for k, tile in enumerate(tiles):
        save(k, *tile).wait()


def field(rows, sgt_block, capacity):
    sources, height, _ = rows.shape
    stations, _, depth, length = sgt_block.shape
    width = WIDTH
    tiles = [(s, start, width) for s in range(stations) for start in range(0, length, width)]
    flops = 2 * sources * capacity * depth * stations * length
    return pl.pallas_call(
        lambda *refs: field_kernel(capacity, tiles, *refs),
        in_specs=[
            pl.BlockSpec(memory_space=pltpu.VMEM),
            pl.BlockSpec(memory_space=pl.ANY),
        ],
        out_specs=pl.BlockSpec(memory_space=pl.ANY),
        out_shape=jax.ShapeDtypeStruct((sources, capacity, stations * length), jnp.bfloat16),
        scratch_shapes=[
            pltpu.VMEM((sources * capacity, depth), jnp.bfloat16),
            pltpu.VMEM((stations, depth, length), jnp.bfloat16),
            pltpu.VMEM((sources, capacity, stations * length), jnp.bfloat16),
            pltpu.SemaphoreType.DMA((len(tiles),)),
            pltpu.SemaphoreType.DMA((len(tiles),)),
        ],
        compiler_params=pltpu.CompilerParams(vmem_limit_bytes=VMEM),
        cost_estimate=pl.CostEstimate(flops=flops, bytes_accessed=sgt_block.size * 2, transcendentals=0),
        name="field_matmul",
    )(rows, sgt_block)


STEP = 64
SPAN = 256
PIECES = 4
PITCH = 9
DEPTH = 2


def plain(taps, seq, k):
    total = taps[0] * seq(k)
    for lag in range(1, len(taps)):
        total = total + taps[lag] * seq(k - lag)
    return total


def halved(seq):
    held = {}

    def both(m):
        if m not in held:
            held[m] = seq(2 * m) + seq(2 * m + 1)
        return held[m]

    return (lambda m: seq(2 * m)), (lambda m: seq(2 * m + 1)), both


def tap_parts(taps):
    even, odd = taps[0::2], taps[1::2]
    return even, odd, [a + b for a, b in zip(even, odd)]


def leaf_taps(taps, depth):
    if depth == 0:
        return taps
    return [value for part in tap_parts(taps) for value in leaf_taps(part, depth - 1)]


def first_carry(taps, seq, depth):
    if depth == 0:
        return []
    parts, seqs = tap_parts(taps), halved(seq)
    found = [plain(parts[1], seqs[1], -1)]
    for part, sub in zip(parts, seqs):
        found += first_carry(part, sub, depth - 1)
    return found


def fast_filter(count, leaf, seq, width, depth, carry, fresh):
    if depth == 0:
        taps = leaf(count)
        return [plain(taps, seq, k) for k in range(width)]
    seqs = halved(seq)
    late = carry.pop(0)
    place = len(fresh)
    fresh.append(None)
    a, b, c = [fast_filter(count // 2, leaf, sub, width // 2, depth - 1, carry, fresh) for sub in seqs]
    fresh[place] = b[-1]
    out = []
    for m in range(width // 2):
        out.append(a[m] + (b[m - 1] if m else late))
        out.append(c[m] - a[m] - b[m])
    return out


def trace_kernel(home_ref, strad_ref, time_ref, part_ref, out_ref, chooser, parts, even, odd, after, done, whole, scales, loaded, saved):
    taps, events = time_ref.shape
    stations, _, length = out_ref.shape
    sources, capacity, _ = part_ref.shape
    slots = sources * capacity
    groups = events // LANES
    count = length // SPAN

    def load(k, s):
        columns = pl.ds(pl.multiple_of(s * length + k * SPAN, LANES), SPAN)
        return pltpu.make_async_copy(part_ref.at[:, :, columns], parts.at[k, s], loaded.at[k])

    def save(k, s):
        columns = pl.ds(pl.multiple_of(k * SPAN, LANES), SPAN)
        return pltpu.make_async_copy(done.at[k, s], out_ref.at[s, :, columns], saved.at[k])

    for k in range(count):
        for s in range(stations):
            load(k, s).start()
    home = jnp.transpose(jnp.broadcast_to(home_ref[...], (LANES, events)))
    strad = jnp.transpose(jnp.broadcast_to(strad_ref[...], (LANES, events)))
    lane = lax.broadcasted_iota(jnp.int32, (events, LANES), 1)
    for k in range(slots // LANES):
        hit = (home == lane + k * LANES) | (strad == lane + k * LANES)
        chooser[:, k * LANES : (k + 1) * LANES] = hit.astype(jnp.float32).astype(jnp.bfloat16)
    for g in range(groups):
        for s in range(stations):
            whole[:, s * groups + g, :] = time_ref[:, g * LANES : (g + 1) * LANES]
    for k, value in enumerate(leaf_taps([whole[k] for k in range(taps)], DEPTH)):
        scales[k] = value

    def gather(k, s, part, target):
        size = events // PIECES
        picked = chooser[part * size : (part + 1) * size, :]
        trace = jnp.dot(picked, parts[k, s].reshape(slots, SPAN), preferred_element_type=jnp.float32)
        for g in range(size // LANES):
            for c in range(SPAN // LANES):
                tile = trace[g * LANES : (g + 1) * LANES, c * LANES : (c + 1) * LANES]
                at = taps + c * LANES
                target[pl.ds(at * PITCH + s * groups + part * (size // LANES) + g, LANES, PITCH), :] = jnp.transpose(tile)

    def seen(ref, start):
        held = {}

        def at(k):
            if k not in held:
                held[k] = ref[pl.ds((start + taps + k) * PITCH, 8), :]
            return held[k]

        return at

    def convolve(ref, step, carry):
        carry, index, fresh = list(carry), [0], []

        def leaf(n):
            index[0] += n
            return [scales[k] for k in range(index[0] - n, index[0])]

        out = fast_filter(taps, leaf, seen(ref, step * STEP), STEP, DEPTH, carry, fresh)
        for k in range(STEP):
            after[pl.ds((step * STEP + k) * PITCH, 8), :] = out[k]
        return fresh

    def finish(k, step):
        at = step * STEP
        for s in range(stations):
            for g in range(groups):
                done[k, s, g * LANES : (g + 1) * LANES, at : at + LANES] = jnp.transpose(
                    after[pl.ds(at * PITCH + s * groups + g, LANES, PITCH), :]
                )

    def wait(k):
        for s in range(stations):
            load(k, s).wait()

    jobs = [(s, part) for s in range(stations) for part in range(PIECES)]
    steps = SPAN // STEP

    def region(k, source, target, carry):
        @pl.when(k + 1 < count)
        def _():
            wait(k + 1)

        for step in range(steps):
            carry = convolve(source, step, carry)
            for s, part in jobs[step * len(jobs) // steps : (step + 1) * len(jobs) // steps]:
                gather(jnp.minimum(k + 1, count - 1), s, part, target)
            if (step + 1) * STEP % LANES == 0:
                finish(k, ((step + 1) * STEP - LANES) // STEP)
        target[: taps * PITCH] = source[SPAN * PITCH : (SPAN + taps) * PITCH]
        for s in range(stations):
            save(k, s).start()
        return carry

    wait(0)
    for s, part in jobs:
        gather(0, s, part, even)
    even[: taps * PITCH] = jnp.zeros((taps * PITCH, LANES), jnp.float32)

    def pair(i, carry):
        carry = region(2 * i, even, odd, carry)
        return tuple(region(2 * i + 1, odd, even, carry))

    silent = first_carry([whole[k] for k in range(taps)], seen(even, 0), DEPTH)
    lax.fori_loop(0, count // 2, pair, tuple(silent))
    for k in range(count):
        for s in range(stations):
            save(k, s).wait()


def traces(home_row, strad_row, source_time, parts, stations):
    taps, events = source_time.shape
    sources, capacity, width = parts.shape
    length = width // stations
    count = length // SPAN
    row = pl.BlockSpec(memory_space=pltpu.VMEM)
    return pl.pallas_call(
        trace_kernel,
        in_specs=[row, row, row, pl.BlockSpec(memory_space=pl.ANY)],
        out_specs=pl.BlockSpec(memory_space=pl.ANY),
        out_shape=jax.ShapeDtypeStruct((stations, events, length), jnp.float32),
        scratch_shapes=[
            pltpu.VMEM((events, sources * capacity), jnp.bfloat16),
            pltpu.VMEM((count, stations, sources, capacity, SPAN), jnp.bfloat16),
            pltpu.VMEM(((taps + SPAN) * PITCH, LANES), jnp.float32),
            pltpu.VMEM(((taps + SPAN) * PITCH, LANES), jnp.float32),
            pltpu.VMEM((SPAN * PITCH, LANES), jnp.float32),
            pltpu.VMEM((count, stations, events, SPAN), jnp.float32),
            pltpu.VMEM((taps, 8, LANES), jnp.float32),
            pltpu.VMEM((taps * 3**DEPTH // 2**DEPTH, 8, LANES), jnp.float32),
            pltpu.SemaphoreType.DMA((count,)),
            pltpu.SemaphoreType.DMA((count,)),
        ],
        compiler_params=pltpu.CompilerParams(vmem_limit_bytes=VMEM),
        name="trace_convolve",
    )(home_row, strad_row, source_time, parts)


def body(sgt_block, weights_home, weights_strad, moment, source_time, home_pos, strad_pos):
    events = weights_home.shape[0]
    blocks = lax.axis_size("blk")
    capacity = 2 * events // blocks
    stations = sgt_block.shape[0]
    home_row = home_pos.reshape(1, events)
    strad_row = strad_pos.reshape(1, events)
    packed = pack(home_row, strad_row, weights_home, weights_strad, moment.T, blocks)
    rows = lax.all_to_all(packed, "blk", split_axis=0, concat_axis=0, tiled=True)
    partial_value = field(rows, sgt_block, capacity)
    returned = lax.all_to_all(partial_value, "blk", split_axis=0, concat_axis=0, tiled=True)
    return traces(home_row, strad_row, source_time.T, returned, stations)


def solution(mesh):
    placed = (
        P("sta", "blk", None, None),
        P("blk", None),
        P("blk", None),
        P("blk", None),
        P("blk", None),
        P("blk"),
        P("blk"),
    )
    return jax.shard_map(
        body, mesh=mesh, in_specs=placed, out_specs=P("sta", "blk", None), check_vma=False
    )
```

time: 157 us -> 116 us (0.74)
  Pallas kernels: 73 us -> 32.1 us
    pallas_call x2, Pallas kernels: 68.8 us -> 28.4 us  [the longest x1 18 us: field(): pl.pallas_call(lambda *refs: field_kernel(capacity, tiles, *refs), in_spe...]
where the time goes in v1:
time: 116 us; the launch traced here: 115 us
  blocking collectives  82.8 us (71%)
  Pallas kernels  32.1 us (28%)
    all_to_all x1, blocking collectives, body(): lax.all_to_all(partial_value, 'blk', split_axis=0, concat_axis=0, tiled=T...  55.9 us
    all_to_all x1, blocking collectives, body(): lax.all_to_all(packed, 'blk', split_axis=0, concat_axis=0, tiled=True)  26.9 us
    pallas_call x1, Pallas kernels, field(): pl.pallas_call(lambda *refs: field_kernel(capacity, tiles, *refs), in_spe...  18 us
    pallas_call x1, Pallas kernels, traces(): pl.pallas_call(trace_kernel, in_specs=[row, row, row, pl.BlockSpec(memory...  10.4 us
    pallas_call x1, Pallas kernels, pack(): pl.pallas_call(lambda *refs: pack_kernel(capacity, *refs), grid=(blocks /...  3.77 us

profile of v1, /device:TPU:0, one launch (start us, length us, event | category | flops | bytes accessed | tf_op | source)
XLA Modules:
  0.0 115.1 jit_solution(1707130523288264984)
XLA Ops:
  0.0 3.8 %pack_rows.1 = bf16[32,136,128]{2,1,0:T(8,128)(2,1)} custom-call(s32[1,512]{1,0:T(1,128)} %bitcast.6, s32[1,512]{1,0:T(1,128)} %bitcast.8, bf16[512,512]{1,0:T(8,128)(2,1)} %refs_2_.1, bf16[512,512]{1,0:T(8,128)(2,1)} %refs_3_.1, bf16[6,512]{1,0:T(8,128)(2,1)} %bitcast.5), custom_call_target="tpu_custom_call" | custom-call | tf_op jit(solution)/shard_map/pack_rows/pallas_call | solution.py:56
  3.8 26.9 %all_to_all.10.refs_0_ = bf16[32,136,128]{2,1,0:T(8,128)(2,1)} all-to-all(bf16[32,136,128]{2,1,0:T(8,128)(2,1)} %pack_rows.1), channel_id=1, replica_groups=mesh['sta'=4,'blk'=32] {'blk'}, dimensions={0} | all-to-all | bytes 2228224 | tf_op jit(solution)/shard_map/all_to_all | solution.py:358
  30.7 18.0 %field_matmul.1 = bf16[32,32,2048]{2,1,0:T(8,128)(2,1)} custom-call(bf16[32,136,128]{2,1,0:T(8,128)(2,1)} %all_to_all.10.refs_0_, bf16[2,1,3072,1024]{3,2,1,0:T(8,128)(2,1)} %refs_1_.1), custom_call_target="tpu_custom_call" | custom-call | flops 12884901888 | bytes 12582912 | tf_op jit(solution)/shard_map/field_matmul/pallas_call | solution.py:128
  48.7 55.9 %all_to_all.11.part_ref = bf16[32,32,2048]{2,1,0:T(8,128)(2,1)} all-to-all(bf16[32,32,2048]{2,1,0:T(8,128)(2,1)} %field_matmul.1), channel_id=1, replica_groups=mesh['sta'=4,'blk'=32] {'blk'}, dimensions={0} | all-to-all | bytes 8388608 | tf_op jit(solution)/shard_map/all_to_all | solution.py:360
  104.6 10.4 %trace_convolve.1 = f32[2,512,1024]{2,1,0:T(8,128)} custom-call(s32[1,512]{1,0:T(1,128)} %bitcast.7, s32[1,512]{1,0:T(1,128)} %bitcast.9, f32[16,512]{1,0:T(8,128)} %bitcast.4, bf16[32,32,2048]{2,1,0:T(8,128)(2,1)} %all_to_all.11.part_ref), custom_call_target="tpu_custom_call" | custom-call | tf_op jit(solution)/shard_map/trace_convolve/pallas_call | solution.py:328

commit v2 on v1

--- a/solution.py
+++ b/solution.py
@@ -9,9 +9,10 @@
 PARTS = 6
 EXTRA = 8
 ROWS = 512
-WIDTH = 256
+WIDTH = 512
 AHEAD = 2
-VMEM = 60 * 1024 * 1024
+VMEM = 44 * 1024 * 1024
+ALL_VMEM = 60 * 1024 * 1024
 
 
 def contract_last(left, right):
@@ -23,9 +24,10 @@
     dests = out_ref.shape[0]
     slots = dests * capacity
     events, points = wh_ref.shape
+    flip = lax.rem(lax.axis_index("blk"), 2) * capacity
     ids = lax.broadcasted_iota(jnp.int32, (slots, events), 0) + step * slots
-    home = (ids == home_ref[...]).astype(jnp.float32).astype(jnp.bfloat16)
-    strad = (ids == strad_ref[...]).astype(jnp.float32).astype(jnp.bfloat16)
+    home = (ids == home_ref[...] ^ flip).astype(jnp.float32).astype(jnp.bfloat16)
+    strad = (ids == strad_ref[...] ^ flip).astype(jnp.float32).astype(jnp.bfloat16)
     rows = jnp.dot(home, wh_ref[...], preferred_element_type=jnp.float32)
     rows = rows + jnp.dot(strad, ws_ref[...], preferred_element_type=jnp.float32)
     rows = rows.astype(jnp.bfloat16)
@@ -65,26 +67,29 @@
         ],
         out_specs=pl.BlockSpec((dests, height, LANES), lambda i: (i, 0, 0)),
         out_shape=jax.ShapeDtypeStruct((blocks, height, LANES), jnp.bfloat16),
-        compiler_params=pltpu.CompilerParams(vmem_limit_bytes=VMEM),
+        compiler_params=pltpu.CompilerParams(vmem_limit_bytes=ALL_VMEM),
         name="pack_rows",
     )(home_row, strad_row, weights_home, weights_strad, moment)
 
 
-def field_kernel(capacity, tiles, rows_ref, sgt_ref, out_ref, combined, field, value, loaded, saved):
-    sources, height, _ = rows_ref.shape
+def field_kernel(capacity, tiles, rows_ref, own_ref, other_ref, out_ref, combined, field, value, loaded, saved):
+    chips, sides, height, _ = rows_ref.shape
     points = (height - EXTRA) // capacity * LANES
-    slots = sources * capacity
-    length = sgt_ref.shape[-1]
-
-    def load(k, s, start, width):
+    slots = chips * capacity
+    length = own_ref.shape[-1]
+
+    def load(k, side, s, start, width):
         columns = pl.ds(start, width)
+        source = other_ref if side else own_ref
         return pltpu.make_async_copy(
-            sgt_ref.at[s, 0, :, columns], field.at[s, :, columns], loaded.at[k]
+            source.at[s, 0, :, columns], field.at[side, s, :, columns], loaded.at[k]
         )
 
-    def save(k, s, start, width):
+    def save(k, side, s, start, width):
         columns = pl.ds(s * length + start, width)
-        return pltpu.make_async_copy(value.at[:, :, columns], out_ref.at[:, :, columns], saved.at[k])
+        return pltpu.make_async_copy(
+            value.at[:, side, :, columns], out_ref.at[:, side, :, columns], saved.at[k]
+        )
 
     for k, tile in enumerate(tiles[:AHEAD]):
         load(k, *tile).start()
@@ -92,58 +97,71 @@
         jnp.int32, (capacity, LANES), 1
     )
     pick = pick.astype(jnp.float32).astype(jnp.bfloat16)
-    packed = rows_ref[:, height - EXTRA :, :].reshape(sources * EXTRA, LANES)
-    moments = contract_last(pick, packed)
-    for m in range(sources):
-        for j in range(points // LANES):
-            weights = rows_ref[m, j * capacity : (j + 1) * capacity, :].astype(jnp.float32)
-            for c in range(PARTS):
-                scale = moments[:, m * EXTRA + c : m * EXTRA + c + 1]
-                at = c * points + j * LANES
-                combined[m * capacity : (m + 1) * capacity, at : at + LANES] = (weights * scale).astype(
-                    jnp.bfloat16
-                )
-    for k, (s, start, width) in enumerate(tiles):
-        load(k, s, start, width).wait()
+
+    def combine(side):
+        packed = rows_ref[:, side, height - EXTRA :, :].reshape(chips * EXTRA, LANES)
+        moments = contract_last(pick, packed)
+        for m in range(chips):
+            for j in range(points // LANES):
+                weights = rows_ref[m, side, j * capacity : (j + 1) * capacity, :].astype(jnp.float32)
+                for c in range(PARTS):
+                    scale = moments[:, m * EXTRA + c : m * EXTRA + c + 1]
+                    at = c * points + j * LANES
+                    combined[side, m * capacity : (m + 1) * capacity, at : at + LANES] = (
+                        weights * scale
+                    ).astype(jnp.bfloat16)
+
+    combine(0)
+    for k, (side, s, start, width) in enumerate(tiles):
+        load(k, side, s, start, width).wait()
         if k + AHEAD < len(tiles):
             load(k + AHEAD, *tiles[k + AHEAD]).start()
+        if k == 1:
+            combine(1)
         for m in range(0, slots, ROWS):
             part = jnp.dot(
-                combined[m : m + ROWS, :], field[s, :, start : start + width], preferred_element_type=jnp.float32
+                combined[side, m : m + ROWS, :],
+                field[side, s, :, start : start + width],
+                preferred_element_type=jnp.float32,
             )
-            value[m // capacity : (m + ROWS) // capacity, :, s * length + start : s * length + start + width] = (
-                part.astype(jnp.bfloat16).reshape(ROWS // capacity, capacity, width)
-            )
-        save(k, s, start, width).start()
+            value[
+                m // capacity : (m + ROWS) // capacity, side, :, s * length + start : s * length + start + width
+            ] = part.astype(jnp.bfloat16).reshape(ROWS // capacity, capacity, width)
+        save(k, side, s, start, width).start()
     for k, tile in enumerate(tiles):
         save(k, *tile).wait()
 
 
-def field(rows, sgt_block, capacity):
-    sources, height, _ = rows.shape
-    stations, _, depth, length = sgt_block.shape
-    width = WIDTH
-    tiles = [(s, start, width) for s in range(stations) for start in range(0, length, width)]
-    flops = 2 * sources * capacity * depth * stations * length
+def field(rows, own, other, capacity):
+    chips, sides, height, _ = rows.shape
+    stations, _, depth, length = own.shape
+    tiles = [
+        (side, s, start, WIDTH)
+        for side in range(sides)
+        for s in range(stations)
+        for start in range(0, length, WIDTH)
+    ]
+    flops = 2 * sides * chips * capacity * depth * stations * length
     return pl.pallas_call(
         lambda *refs: field_kernel(capacity, tiles, *refs),
         in_specs=[
             pl.BlockSpec(memory_space=pltpu.VMEM),
             pl.BlockSpec(memory_space=pl.ANY),
+            pl.BlockSpec(memory_space=pl.ANY),
         ],
         out_specs=pl.BlockSpec(memory_space=pl.ANY),
-        out_shape=jax.ShapeDtypeStruct((sources, capacity, stations * length), jnp.bfloat16),
+        out_shape=jax.ShapeDtypeStruct((chips, sides, capacity, stations * length), jnp.bfloat16),
         scratch_shapes=[
-            pltpu.VMEM((sources * capacity, depth), jnp.bfloat16),
-            pltpu.VMEM((stations, depth, length), jnp.bfloat16),
-            pltpu.VMEM((sources, capacity, stations * length), jnp.bfloat16),
+            pltpu.VMEM((sides, chips * capacity, depth), jnp.bfloat16),
+            pltpu.VMEM((sides, stations, depth, length), jnp.bfloat16),
+            pltpu.VMEM((chips, sides, capacity, stations * length), jnp.bfloat16),
             pltpu.SemaphoreType.DMA((len(tiles),)),
             pltpu.SemaphoreType.DMA((len(tiles),)),
         ],
         compiler_params=pltpu.CompilerParams(vmem_limit_bytes=VMEM),
-        cost_estimate=pl.CostEstimate(flops=flops, bytes_accessed=sgt_block.size * 2, transcendentals=0),
+        cost_estimate=pl.CostEstimate(flops=flops, bytes_accessed=own.size * 4, transcendentals=0),
         name="field_matmul",
-    )(rows, sgt_block)
+    )(rows, own, other)
 
 
 STEP = 64
@@ -228,8 +246,9 @@
     for k in range(count):
         for s in range(stations):
             load(k, s).start()
-    home = jnp.transpose(jnp.broadcast_to(home_ref[...], (LANES, events)))
-    strad = jnp.transpose(jnp.broadcast_to(strad_ref[...], (LANES, events)))
+    flip = lax.rem(lax.axis_index("blk"), 2) * capacity
+    home = jnp.transpose(jnp.broadcast_to(home_ref[...] ^ flip, (LANES, events)))
+    strad = jnp.transpose(jnp.broadcast_to(strad_ref[...] ^ flip, (LANES, events)))
     lane = lax.broadcasted_iota(jnp.int32, (events, LANES), 1)
     for k in range(slots // LANES):
         hit = (home == lane + k * LANES) | (strad == lane + k * LANES)
@@ -350,14 +369,23 @@
 def body(sgt_block, weights_home, weights_strad, moment, source_time, home_pos, strad_pos):
     events = weights_home.shape[0]
     blocks = lax.axis_size("blk")
+    chips = blocks // 2
     capacity = 2 * events // blocks
     stations = sgt_block.shape[0]
     home_row = home_pos.reshape(1, events)
     strad_row = strad_pos.reshape(1, events)
+    same_core = [[2 * k + core for k in range(chips)] for core in range(2)]
+
+    def exchange(value):
+        return lax.all_to_all(
+            value, "blk", split_axis=0, concat_axis=0, tiled=True, axis_index_groups=same_core
+        )
+
+    other = lax.ppermute(sgt_block, "blk", [(i, i ^ 1) for i in range(blocks)])
     packed = pack(home_row, strad_row, weights_home, weights_strad, moment.T, blocks)
-    rows = lax.all_to_all(packed, "blk", split_axis=0, concat_axis=0, tiled=True)
-    partial_value = field(rows, sgt_block, capacity)
-    returned = lax.all_to_all(partial_value, "blk", split_axis=0, concat_axis=0, tiled=True)
+    rows = exchange(packed.reshape((chips, 2) + packed.shape[1:]))
+    returned = exchange(field(rows, sgt_block, other, capacity))
+    returned = returned.reshape(blocks, capacity, returned.shape[-1])
     return traces(home_row, strad_row, source_time.T, returned, stations)
 
 

time: 116 us -> 111 us (0.957)
  blocking collectives: 82.8 us -> 80.4 us
  Pallas kernels: 32.1 us -> 30.3 us
    all_to_all x2, blocking collectives: 82.8 us -> 80.4 us  [exchange(): lax.all_to_all(value, 'blk', split_axis=0, concat_axis=0, tiled=True, axi...]
  transfers between devices with their start and end apart: 0 -> 1, of which waited for: 0 -> 0; matrix products, arithmetic and copies ran while one was open for 0% -> 0% of each run, Pallas kernels for 0% -> 3%
where the time goes in v2:
time: 111 us
  blocking collectives  80.4 us (72%)
  Pallas kernels  30.3 us (27%)
    all_to_all x2, blocking collectives, exchange(): lax.all_to_all(value, 'blk', split_axis=0, concat_axis=0, tiled=True, axi...  80.4 us
    pallas_call x1, Pallas kernels, field(): pl.pallas_call(lambda *refs: field_kernel(capacity, tiles, *refs), in_spe...  17.1 us
    pallas_call x1, Pallas kernels, traces(): pl.pallas_call(trace_kernel, in_specs=[row, row, row, pl.BlockSpec(memory...  9.51 us
    pallas_call x1, Pallas kernels, pack(): pl.pallas_call(lambda *refs: pack_kernel(capacity, *refs), grid=(blocks /...  3.75 us
  transfers between devices with their start and end apart: 1, of which 0 were waited for; matrix products, arithmetic and copies ran while one was open for 0% of the time, Pallas kernels for 3%

profile of v2, /device:TPU:0, one launch (start us, length us, event | category | flops | bytes accessed | tf_op | source)
XLA Modules:
  0.0 111.0 jit_solution(6213042867035096552)
XLA Ops:
  0.0 0.0 collective-permute-start
  0.0 3.7 %pack_rows.1 = bf16[32,136,128]{2,1,0:T(8,128)(2,1)} custom-call(s32[1,512]{1,0:T(1,128)} %bitcast.8, s32[1,512]{1,0:T(1,128)} %bitcast.10, bf16[512,512]{1,0:T(8,128)(2,1)} %refs_2_.1, bf16[512,512]{1,0:T(8,128)(2,1)} %refs_3_.1, bf16[6,512]{1,0:T(8,128)(2,1)} %bitcast.13), custom_call_target="tpu_custom_call" | custom-call | tf_op jit(solution)/shard_map/pack_rows/pallas_call | solution.py:58
  3.8 26.6 %all_to_all.10.refs_0_ = bf16[16,2,136,128]{3,2,1,0:T(8,128)(2,1)S(1)} all-to-all(bf16[16,2,136,128]{3,2,1,0:T(8,128)(2,1)} %bitcast.12), channel_id=1, replica_groups={{0,2,4,6,8,10,12,14,16,18,20,22,24,26,28,30},{1,3,5,7,9,11,13,15,17,19,..., dimensions={0} | all-to-all | bytes 2228224 | tf_op jit(solution)/shard_map/all_to_all | solution.py:380
  30.3 0.0 collective-permute-done.refs_2_
  30.3 17.1 %field_matmul.1 = bf16[16,2,32,2048]{3,2,1,0:T(8,128)(2,1)S(1)} custom-call(bf16[16,2,136,128]{3,2,1,0:T(8,128)(2,1)S(1)} %all_to_all.10.refs_0_, bf16[2,1,3072,1024]{3,2,1,0:T(8,128)(2,1)} %refs_1_.1, bf16[2,1,3072,1024]{3,2,1,0:T(8,128)(2,1)} %collective-permute-done.refs_2_), custom_call_target="tpu_custom_call" | custom-call | flops 12884901888 | bytes 25165824 | tf_op jit(solution)/shard_map/field_matmul/pallas_call | solution.py:145
  47.4 0.0 copy-start
  47.4 0.0 copy-start.1
  47.4 0.0 copy-start.2
  47.4 53.8 %all_to_all.11 = bf16[16,2,32,2048]{3,2,1,0:T(8,128)(2,1)S(1)} all-to-all(bf16[16,2,32,2048]{3,2,1,0:T(8,128)(2,1)S(1)} %field_matmul.1), channel_id=1, replica_groups={{0,2,4,6,8,10,12,14,16,18,20,22,24,26,28,30},{1,3,5,7,9,11,13,15,17,19,..., dimensions={0} | all-to-all | bytes 8388608 | tf_op jit(solution)/shard_map/all_to_all | solution.py:380
  101.3 0.0 copy-done
  101.3 0.0 copy-done.1
  101.3 0.0 copy-done.2
  101.3 9.5 %trace_convolve.1 = f32[2,512,1024]{2,1,0:T(8,128)} custom-call(s32[1,512]{1,0:T(1,128)S(1)} %bitcast.9, s32[1,512]{1,0:T(1,128)S(1)} %bitcast.11, f32[16,512]{1,0:T(8,128)S(1)} %bitcast.7, bf16[32,32,2048]{2,1,0:T(8,128)(2,1)S(1)} %bitcast.6), custom_call_target="tpu_custom_call" | custom-call | tf_op jit(solution)/shard_map/trace_convolve/pallas_call | solution.py:347
Async XLA Ops:
  0.0 30.3 %collective-permute-start = (bf16[2,1,3072,1024]{3,2,1,0:T(8,128)(2,1)}, bf16[2,1,3072,1024]{3,2,1,0:T(8,128)(2,1)}, u32[]{:S(2)}, u32[]{:S(2)}) collective-permute-start(bf16[2,1,3072,1024]{3,2,1,0:T(8,128)(2,1)} %refs_1_.1), channel_id=1, source_target_pairs={{0,1},{1,0},{2,3},{3,2},{4,5},{5,4},{6,7},{7,6},{8,9},{9,8},{10,11... | collective-permute-start | bytes 37748744 | tf_op jit(solution)/shard_map/ppermute | solution.py:384
  47.4 53.9 %copy-start = (f32[512,16]{0,1:T(8,128)S(1)}, f32[512,16]{0,1:T(8,128)}, u32[]{:S(2)}) copy-start(f32[512,16]{0,1:T(8,128)} %param.11) | copy-start | bytes 98308
  47.4 53.9 %copy-start.1 = (s32[512]{0:T(512)S(1)}, s32[512]{0:T(512)}, u32[]{:S(2)}) copy-start(s32[512]{0:T(512)} %param.12) | copy-start | bytes 6148
  47.4 53.9 %copy-start.2 = (s32[512]{0:T(512)S(1)}, s32[512]{0:T(512)}, u32[]{:S(2)}) copy-start(s32[512]{0:T(512)} %param.13) | copy-start | bytes 6148

commit v3 on v2

--- a/solution.py
+++ b/solution.py
@@ -72,7 +72,10 @@
     )(home_row, strad_row, weights_home, weights_strad, moment)
 
 
-def field_kernel(capacity, tiles, rows_ref, own_ref, other_ref, out_ref, combined, field, value, loaded, saved):
+def field_kernel(
+    capacity, tiles, rows_ref, own_ref, other_ref, home_ref, strad_ref, time_ref,
+    out_ref, chooser, scales, combined, field, loaded,
+):
     chips, sides, height, _ = rows_ref.shape
     points = (height - EXTRA) // capacity * LANES
     slots = chips * capacity
@@ -83,12 +86,6 @@
         source = other_ref if side else own_ref
         return pltpu.make_async_copy(
             source.at[s, 0, :, columns], field.at[side, s, :, columns], loaded.at[k]
-        )
-
-    def save(k, side, s, start, width):
-        columns = pl.ds(s * length + start, width)
-        return pltpu.make_async_copy(
-            value.at[:, side, :, columns], out_ref.at[:, side, :, columns], saved.at[k]
         )
 
     for k, tile in enumerate(tiles[:AHEAD]):
@@ -111,6 +108,29 @@
                         weights * scale
                     ).astype(jnp.bfloat16)
 
+    events = time_ref.shape[1]
+    groups = events // LANES
+    stations = own_ref.shape[0]
+    flip = lax.rem(lax.axis_index("blk"), 2) * capacity
+
+    def choose(first, last):
+        home = jnp.transpose(jnp.broadcast_to(home_ref[...] ^ flip, (LANES, events)))
+        strad = jnp.transpose(jnp.broadcast_to(strad_ref[...] ^ flip, (LANES, events)))
+        lane = lax.broadcasted_iota(jnp.int32, (events, LANES), 1)
+        for k in range(first, last):
+            hit = (home == lane + k * LANES) | (strad == lane + k * LANES)
+            chooser[:, k * LANES : (k + 1) * LANES] = hit.astype(jnp.float32).astype(jnp.bfloat16)
+
+    def spread_taps():
+        taps = [
+            jnp.concatenate(
+                [time_ref[k : k + 1, g * LANES : (g + 1) * LANES] for g in range(groups)] * stations, axis=0
+            )
+            for k in range(time_ref.shape[0])
+        ]
+        for k, leaf in enumerate(leaf_taps(taps, DEPTH)):
+            scales[k] = leaf
+
     combine(0)
     for k, (side, s, start, width) in enumerate(tiles):
         load(k, side, s, start, width).wait()
@@ -118,23 +138,26 @@
             load(k + AHEAD, *tiles[k + AHEAD]).start()
         if k == 1:
             combine(1)
+        if 2 <= k < 6:
+            pieces = chooser.shape[1] // LANES
+            choose((k - 2) * pieces // 4, (k - 1) * pieces // 4)
+        if k == 6:
+            spread_taps()
         for m in range(0, slots, ROWS):
             part = jnp.dot(
                 combined[side, m : m + ROWS, :],
                 field[side, s, :, start : start + width],
                 preferred_element_type=jnp.float32,
             )
-            value[
+            out_ref[
                 m // capacity : (m + ROWS) // capacity, side, :, s * length + start : s * length + start + width
             ] = part.astype(jnp.bfloat16).reshape(ROWS // capacity, capacity, width)
-        save(k, side, s, start, width).start()
-    for k, tile in enumerate(tiles):
-        save(k, *tile).wait()
-
-
-def field(rows, own, other, capacity):
+
+
+def field(rows, own, other, home_row, strad_row, source_time, capacity):
     chips, sides, height, _ = rows.shape
     stations, _, depth, length = own.shape
+    taps, events = source_time.shape
     tiles = [
         (side, s, start, WIDTH)
         for side in range(sides)
@@ -148,20 +171,25 @@
             pl.BlockSpec(memory_space=pltpu.VMEM),
             pl.BlockSpec(memory_space=pl.ANY),
             pl.BlockSpec(memory_space=pl.ANY),
-        ],
-        out_specs=pl.BlockSpec(memory_space=pl.ANY),
-        out_shape=jax.ShapeDtypeStruct((chips, sides, capacity, stations * length), jnp.bfloat16),
+            pl.BlockSpec(memory_space=pltpu.VMEM),
+            pl.BlockSpec(memory_space=pltpu.VMEM),
+            pl.BlockSpec(memory_space=pltpu.VMEM),
+        ],
+        out_specs=[pl.BlockSpec(memory_space=pltpu.VMEM)] * 3,
+        out_shape=[
+            jax.ShapeDtypeStruct((chips, sides, capacity, stations * length), jnp.bfloat16),
+            jax.ShapeDtypeStruct((events, chips * sides * capacity), jnp.bfloat16),
+            jax.ShapeDtypeStruct((taps * 3**DEPTH // 2**DEPTH, 8, LANES), jnp.float32),
+        ],
         scratch_shapes=[
             pltpu.VMEM((sides, chips * capacity, depth), jnp.bfloat16),
             pltpu.VMEM((sides, stations, depth, length), jnp.bfloat16),
-            pltpu.VMEM((chips, sides, capacity, stations * length), jnp.bfloat16),
-            pltpu.SemaphoreType.DMA((len(tiles),)),
             pltpu.SemaphoreType.DMA((len(tiles),)),
         ],
         compiler_params=pltpu.CompilerParams(vmem_limit_bytes=VMEM),
         cost_estimate=pl.CostEstimate(flops=flops, bytes_accessed=own.size * 4, transcendentals=0),
         name="field_matmul",
-    )(rows, own, other)
+    )(rows, own, other, home_row, strad_row, source_time)
 
 
 STEP = 64
@@ -198,16 +226,6 @@
     if depth == 0:
         return taps
     return [value for part in tap_parts(taps) for value in leaf_taps(part, depth - 1)]
-
-
-def first_carry(taps, seq, depth):
-    if depth == 0:
-        return []
-    parts, seqs = tap_parts(taps), halved(seq)
-    found = [plain(parts[1], seqs[1], -1)]
-    for part, sub in zip(parts, seqs):
-        found += first_carry(part, sub, depth - 1)
-    return found
 
 
 def fast_filter(count, leaf, seq, width, depth, carry, fresh):
@@ -227,42 +245,24 @@
     return out
 
 
-def trace_kernel(home_ref, strad_ref, time_ref, part_ref, out_ref, chooser, parts, even, odd, after, done, whole, scales, loaded, saved):
-    taps, events = time_ref.shape
+def trace_kernel(taps, chooser, scales, part_ref, out_ref, even, odd, after, done, saved):
+    events = chooser.shape[0]
     stations, _, length = out_ref.shape
     sources, capacity, _ = part_ref.shape
     slots = sources * capacity
     groups = events // LANES
     count = length // SPAN
 
-    def load(k, s):
-        columns = pl.ds(pl.multiple_of(s * length + k * SPAN, LANES), SPAN)
-        return pltpu.make_async_copy(part_ref.at[:, :, columns], parts.at[k, s], loaded.at[k])
-
     def save(k, s):
         columns = pl.ds(pl.multiple_of(k * SPAN, LANES), SPAN)
         return pltpu.make_async_copy(done.at[k, s], out_ref.at[s, :, columns], saved.at[k])
 
-    for k in range(count):
-        for s in range(stations):
-            load(k, s).start()
-    flip = lax.rem(lax.axis_index("blk"), 2) * capacity
-    home = jnp.transpose(jnp.broadcast_to(home_ref[...] ^ flip, (LANES, events)))
-    strad = jnp.transpose(jnp.broadcast_to(strad_ref[...] ^ flip, (LANES, events)))
-    lane = lax.broadcasted_iota(jnp.int32, (events, LANES), 1)
-    for k in range(slots // LANES):
-        hit = (home == lane + k * LANES) | (strad == lane + k * LANES)
-        chooser[:, k * LANES : (k + 1) * LANES] = hit.astype(jnp.float32).astype(jnp.bfloat16)
-    for g in range(groups):
-        for s in range(stations):
-            whole[:, s * groups + g, :] = time_ref[:, g * LANES : (g + 1) * LANES]
-    for k, value in enumerate(leaf_taps([whole[k] for k in range(taps)], DEPTH)):
-        scales[k] = value
-
     def gather(k, s, part, target):
         size = events // PIECES
         picked = chooser[part * size : (part + 1) * size, :]
-        trace = jnp.dot(picked, parts[k, s].reshape(slots, SPAN), preferred_element_type=jnp.float32)
+        columns = pl.ds(pl.multiple_of(s * length + k * SPAN, LANES), SPAN)
+        values = part_ref[:, :, columns].reshape(slots, SPAN)
+        trace = jnp.dot(picked, values, preferred_element_type=jnp.float32)
         for g in range(size // LANES):
             for c in range(SPAN // LANES):
                 tile = trace[g * LANES : (g + 1) * LANES, c * LANES : (c + 1) * LANES]
@@ -299,18 +299,10 @@
                     after[pl.ds(at * PITCH + s * groups + g, LANES, PITCH), :]
                 )
 
-    def wait(k):
-        for s in range(stations):
-            load(k, s).wait()
-
     jobs = [(s, part) for s in range(stations) for part in range(PIECES)]
     steps = SPAN // STEP
 
     def region(k, source, target, carry):
-        @pl.when(k + 1 < count)
-        def _():
-            wait(k + 1)
-
         for step in range(steps):
             carry = convolve(source, step, carry)
             for s, part in jobs[step * len(jobs) // steps : (step + 1) * len(jobs) // steps]:
@@ -322,7 +314,6 @@
             save(k, s).start()
         return carry
 
-    wait(0)
     for s, part in jobs:
         gather(0, s, part, even)
     even[: taps * PITCH] = jnp.zeros((taps * PITCH, LANES), jnp.float32)
@@ -331,39 +322,34 @@
         carry = region(2 * i, even, odd, carry)
         return tuple(region(2 * i + 1, odd, even, carry))
 
-    silent = first_carry([whole[k] for k in range(taps)], seen(even, 0), DEPTH)
-    lax.fori_loop(0, count // 2, pair, tuple(silent))
+    silent = jnp.zeros((8, LANES), jnp.float32)
+    lax.fori_loop(0, count // 2, pair, (silent,) * ((3**DEPTH - 1) // 2))
     for k in range(count):
         for s in range(stations):
             save(k, s).wait()
 
 
-def traces(home_row, strad_row, source_time, parts, stations):
-    taps, events = source_time.shape
+def traces(chooser, scales, parts, taps, stations):
+    events = chooser.shape[0]
     sources, capacity, width = parts.shape
     length = width // stations
     count = length // SPAN
-    row = pl.BlockSpec(memory_space=pltpu.VMEM)
+    held = pl.BlockSpec(memory_space=pltpu.VMEM)
     return pl.pallas_call(
-        trace_kernel,
-        in_specs=[row, row, row, pl.BlockSpec(memory_space=pl.ANY)],
+        lambda *refs: trace_kernel(taps, *refs),
+        in_specs=[held, held, held],
         out_specs=pl.BlockSpec(memory_space=pl.ANY),
         out_shape=jax.ShapeDtypeStruct((stations, events, length), jnp.float32),
         scratch_shapes=[
-            pltpu.VMEM((events, sources * capacity), jnp.bfloat16),
-            pltpu.VMEM((count, stations, sources, capacity, SPAN), jnp.bfloat16),
             pltpu.VMEM(((taps + SPAN) * PITCH, LANES), jnp.float32),
             pltpu.VMEM(((taps + SPAN) * PITCH, LANES), jnp.float32),
             pltpu.VMEM((SPAN * PITCH, LANES), jnp.float32),
             pltpu.VMEM((count, stations, events, SPAN), jnp.float32),
-            pltpu.VMEM((taps, 8, LANES), jnp.float32),
-            pltpu.VMEM((taps * 3**DEPTH // 2**DEPTH, 8, LANES), jnp.float32),
-            pltpu.SemaphoreType.DMA((count,)),
             pltpu.SemaphoreType.DMA((count,)),
         ],
         compiler_params=pltpu.CompilerParams(vmem_limit_bytes=VMEM),
         name="trace_convolve",
-    )(home_row, strad_row, source_time, parts)
+    )(chooser, scales, parts)
 
 
 def body(sgt_block, weights_home, weights_strad, moment, source_time, home_pos, strad_pos):
@@ -384,9 +370,12 @@
     other = lax.ppermute(sgt_block, "blk", [(i, i ^ 1) for i in range(blocks)])
     packed = pack(home_row, strad_row, weights_home, weights_strad, moment.T, blocks)
     rows = exchange(packed.reshape((chips, 2) + packed.shape[1:]))
-    returned = exchange(field(rows, sgt_block, other, capacity))
+    partial_value, chooser, scales = field(
+        rows, sgt_block, other, home_row, strad_row, source_time.T, capacity
+    )
+    returned = exchange(partial_value)
     returned = returned.reshape(blocks, capacity, returned.shape[-1])
-    return traces(home_row, strad_row, source_time.T, returned, stations)
+    return traces(chooser, scales, returned, source_time.shape[1], stations)
 
 
 def solution(mesh):

time: 111 us -> 109 us (0.982)
  Pallas kernels: 30.3 us -> 28.5 us
    pallas_call x1, Pallas kernels: 9.51 us -> 8.09 us  [traces(): pl.pallas_call(lambda *refs: trace_kernel(taps, *refs), in_specs=[held, h...]
where the time goes in v3:
time: 109 us
  blocking collectives  80.3 us (74%)
  Pallas kernels  28.5 us (26%)
    all_to_all x2, blocking collectives, exchange(): lax.all_to_all(value, 'blk', split_axis=0, concat_axis=0, tiled=True, axi...  80.3 us
    pallas_call x1, Pallas kernels, field(): pl.pallas_call(lambda *refs: field_kernel(capacity, tiles, *refs), in_spe...  16.6 us
    pallas_call x1, Pallas kernels, traces(): pl.pallas_call(lambda *refs: trace_kernel(taps, *refs), in_specs=[held, h...  8.09 us
    pallas_call x1, Pallas kernels, pack(): pl.pallas_call(lambda *refs: pack_kernel(capacity, *refs), grid=(blocks /...  3.78 us
  transfers between devices with their start and end apart: 1, of which 0 were waited for; matrix products, arithmetic and copies ran while one was open for 0% of the time, Pallas kernels for 3%

profile of v3, /device:TPU:0, one launch (start us, length us, event | category | flops | bytes accessed | tf_op | source)
XLA Modules:
  0.0 109.0 jit_solution(15155011138286470783)
XLA Ops:
  0.0 0.0 copy-start.1
  0.0 0.0 copy-start
  0.0 0.0 copy-start.2
  0.0 0.0 collective-permute-start
  0.0 3.8 %pack_rows.1 = bf16[32,136,128]{2,1,0:T(8,128)(2,1)} custom-call(s32[1,512]{1,0:T(1,128)} %bitcast.7, s32[1,512]{1,0:T(1,128)} %bitcast.9, bf16[512,512]{1,0:T(8,128)(2,1)} %refs_2_.1, bf16[512,512]{1,0:T(8,128)(2,1)} %refs_3_.1, bf16[6,512]{1,0:T(8,128)(2,1)} %bitcast.13), custom_call_target="tpu_custom_call" | custom-call | tf_op jit(solution)/shard_map/pack_rows/pallas_call | solution.py:58
  3.8 26.6 %all_to_all.10.refs_0_ = bf16[16,2,136,128]{3,2,1,0:T(8,128)(2,1)S(1)} all-to-all(bf16[16,2,136,128]{3,2,1,0:T(8,128)(2,1)} %bitcast.12), channel_id=1, replica_groups={{0,2,4,6,8,10,12,14,16,18,20,22,24,26,28,30},{1,3,5,7,9,11,13,15,17,19,..., dimensions={0} | all-to-all | bytes 2228224 | tf_op jit(solution)/shard_map/all_to_all | solution.py:366
  30.4 0.0 collective-permute-done.refs_2_
  30.4 0.0 copy-done.1
  30.4 0.0 copy-done
  30.4 0.0 copy-done.2
  30.4 16.6 %field_matmul.1 = (bf16[16,2,32,2048]{3,2,1,0:T(8,128)(2,1)S(1)}, bf16[512,1024]{1,0:T(8,128)(2,1)S(1)}, f32[36,8,128]{2,1,0:T(8,128)S(1)}) custom-call(bf16[16,2,136,128]{3,2,1,0:T(8,128)(2,1)S(1)} %all_to_all.10.refs_0_, bf16[2,1,3072,1024]{3,2,1,0:T(8,128)(2,1)} %refs_1_.1, bf16[2,1,3072,1024]{3,2,1,0:T(8,128)(2,1)} %collective-permute-done.refs_2_, ...), custom_call_target="tpu_custom_call" | custom-call | flops 12884901888 | bytes 25165824 | tf_op jit(solution)/shard_map/field_matmul/pallas_call | solution.py:168
  47.0 53.7 %all_to_all.11 = bf16[16,2,32,2048]{3,2,1,0:T(8,128)(2,1)S(1)} all-to-all(bf16[16,2,32,2048]{3,2,1,0:T(8,128)(2,1)S(1)} %get-tuple-element.10), channel_id=1, replica_groups={{0,2,4,6,8,10,12,14,16,18,20,22,24,26,28,30},{1,3,5,7,9,11,13,15,17,19,..., dimensions={0} | all-to-all | bytes 8388608 | tf_op jit(solution)/shard_map/all_to_all | solution.py:366
  100.7 8.1 %trace_convolve.1 = f32[2,512,1024]{2,1,0:T(8,128)} custom-call(bf16[512,1024]{1,0:T(8,128)(2,1)S(1)} %get-tuple-element.8.refs_0_, f32[36,8,128]{2,1,0:T(8,128)S(1)} %get-tuple-element.9.refs_1_, bf16[32,32,2048]{2,1,0:T(8,128)(2,1)S(1)} %bitcast.6), custom_call_target="tpu_custom_call" | custom-call | tf_op jit(solution)/shard_map/trace_convolve/pallas_call | solution.py:338
Async XLA Ops:
  0.0 30.4 %copy-start.1 = (s32[512]{0:T(512)S(1)}, s32[512]{0:T(512)}, u32[]{:S(2)}) copy-start(s32[512]{0:T(512)} %param.13) | copy-start | bytes 6148
  0.0 30.4 %copy-start = (s32[512]{0:T(512)S(1)}, s32[512]{0:T(512)}, u32[]{:S(2)}) copy-start(s32[512]{0:T(512)} %param.12) | copy-start | bytes 6148
  0.0 30.4 %copy-start.2 = (f32[512,16]{0,1:T(8,128)S(1)}, f32[512,16]{0,1:T(8,128)}, u32[]{:S(2)}) copy-start(f32[512,16]{0,1:T(8,128)} %param.11) | copy-start | bytes 98308
  0.0 30.4 %collective-permute-start = (bf16[2,1,3072,1024]{3,2,1,0:T(8,128)(2,1)}, bf16[2,1,3072,1024]{3,2,1,0:T(8,128)(2,1)}, u32[]{:S(2)}, u32[]{:S(2)}) collective-permute-start(bf16[2,1,3072,1024]{3,2,1,0:T(8,128)(2,1)} %refs_1_.1), channel_id=1, source_target_pairs={{0,1},{1,0},{2,3},{3,2},{4,5},{5,4},{6,7},{7,6},{8,9},{9,8},{10,11... | collective-permute-start | bytes 37748744 | tf_op jit(solution)/shard_map/ppermute | solution.py:370

commit v4 on v3

--- a/solution.py
+++ b/solution.py
@@ -341,9 +341,9 @@
         out_specs=pl.BlockSpec(memory_space=pl.ANY),
         out_shape=jax.ShapeDtypeStruct((stations, events, length), jnp.float32),
         scratch_shapes=[
-            pltpu.VMEM(((taps + SPAN) * PITCH, LANES), jnp.float32),
-            pltpu.VMEM(((taps + SPAN) * PITCH, LANES), jnp.float32),
-            pltpu.VMEM((SPAN * PITCH, LANES), jnp.float32),
+            pltpu.VMEM(((taps + SPAN + 1) * PITCH, LANES), jnp.float32),
+            pltpu.VMEM(((taps + SPAN + 1) * PITCH, LANES), jnp.float32),
+            pltpu.VMEM(((SPAN + 1) * PITCH, LANES), jnp.float32),
             pltpu.VMEM((count, stations, events, SPAN), jnp.float32),
             pltpu.SemaphoreType.DMA((count,)),
         ],

time: 109 us -> 109 us (level)
  no operation moved by 1% of the time
where the time goes in v4:
time: 109 us
  blocking collectives  80.3 us (74%)
  Pallas kernels  28.4 us (26%)
    all_to_all x2, blocking collectives, exchange(): lax.all_to_all(value, 'blk', split_axis=0, concat_axis=0, tiled=True, axi...  80.3 us
    pallas_call x1, Pallas kernels, field(): pl.pallas_call(lambda *refs: field_kernel(capacity, tiles, *refs), in_spe...  16.6 us
    pallas_call x1, Pallas kernels, traces(): pl.pallas_call(lambda *refs: trace_kernel(taps, *refs), in_specs=[held, h...  8.06 us
    pallas_call x1, Pallas kernels, pack(): pl.pallas_call(lambda *refs: pack_kernel(capacity, *refs), grid=(blocks /...  3.78 us
  transfers between devices with their start and end apart: 1, of which 0 were waited for; matrix products, arithmetic and copies ran while one was open for 0% of the time, Pallas kernels for 3%

profile of v4, /device:TPU:0, one launch (start us, length us, event | category | flops | bytes accessed | tf_op | source)
XLA Modules:
  0.0 108.9 jit_solution(17640933400935736428)
XLA Ops:
  0.0 0.0 copy-start.1
  0.0 0.0 copy-start
  0.0 0.0 copy-start.2
  0.0 0.0 collective-permute-start
  0.0 3.8 %pack_rows.1 = bf16[32,136,128]{2,1,0:T(8,128)(2,1)} custom-call(s32[1,512]{1,0:T(1,128)} %bitcast.7, s32[1,512]{1,0:T(1,128)} %bitcast.9, bf16[512,512]{1,0:T(8,128)(2,1)} %refs_2_.1, bf16[512,512]{1,0:T(8,128)(2,1)} %refs_3_.1, bf16[6,512]{1,0:T(8,128)(2,1)} %bitcast.13), custom_call_target="tpu_custom_call" | custom-call | tf_op jit(solution)/shard_map/pack_rows/pallas_call | solution.py:58
  3.8 26.6 %all_to_all.10.refs_0_ = bf16[16,2,136,128]{3,2,1,0:T(8,128)(2,1)S(1)} all-to-all(bf16[16,2,136,128]{3,2,1,0:T(8,128)(2,1)} %bitcast.12), channel_id=1, replica_groups={{0,2,4,6,8,10,12,14,16,18,20,22,24,26,28,30},{1,3,5,7,9,11,13,15,17,19,..., dimensions={0} | all-to-all | bytes 2228224 | tf_op jit(solution)/shard_map/all_to_all | solution.py:366
  30.4 0.0 collective-permute-done.refs_2_
  30.4 0.0 copy-done.1
  30.4 0.0 copy-done
  30.4 0.0 copy-done.2
  30.4 16.6 %field_matmul.1 = (bf16[16,2,32,2048]{3,2,1,0:T(8,128)(2,1)S(1)}, bf16[512,1024]{1,0:T(8,128)(2,1)S(1)}, f32[36,8,128]{2,1,0:T(8,128)S(1)}) custom-call(bf16[16,2,136,128]{3,2,1,0:T(8,128)(2,1)S(1)} %all_to_all.10.refs_0_, bf16[2,1,3072,1024]{3,2,1,0:T(8,128)(2,1)} %refs_1_.1, bf16[2,1,3072,1024]{3,2,1,0:T(8,128)(2,1)} %collective-permute-done.refs_2_, ...), custom_call_target="tpu_custom_call" | custom-call | flops 12884901888 | bytes 25165824 | tf_op jit(solution)/shard_map/field_matmul/pallas_call | solution.py:168
  47.0 53.7 %all_to_all.11 = bf16[16,2,32,2048]{3,2,1,0:T(8,128)(2,1)S(1)} all-to-all(bf16[16,2,32,2048]{3,2,1,0:T(8,128)(2,1)S(1)} %get-tuple-element.10), channel_id=1, replica_groups={{0,2,4,6,8,10,12,14,16,18,20,22,24,26,28,30},{1,3,5,7,9,11,13,15,17,19,..., dimensions={0} | all-to-all | bytes 8388608 | tf_op jit(solution)/shard_map/all_to_all | solution.py:366
  100.7 8.1 %trace_convolve.1 = f32[2,512,1024]{2,1,0:T(8,128)} custom-call(bf16[512,1024]{1,0:T(8,128)(2,1)S(1)} %get-tuple-element.8.refs_0_, f32[36,8,128]{2,1,0:T(8,128)S(1)} %get-tuple-element.9.refs_1_, bf16[32,32,2048]{2,1,0:T(8,128)(2,1)S(1)} %bitcast.6), custom_call_target="tpu_custom_call" | custom-call | tf_op jit(solution)/shard_map/trace_convolve/pallas_call | solution.py:338
Async XLA Ops:
  0.0 30.4 %copy-start.1 = (s32[512]{0:T(512)S(1)}, s32[512]{0:T(512)}, u32[]{:S(2)}) copy-start(s32[512]{0:T(512)} %param.13) | copy-start | bytes 6148
  0.0 30.4 %copy-start = (s32[512]{0:T(512)S(1)}, s32[512]{0:T(512)}, u32[]{:S(2)}) copy-start(s32[512]{0:T(512)} %param.12) | copy-start | bytes 6148
  0.0 30.4 %copy-start.2 = (f32[512,16]{0,1:T(8,128)S(1)}, f32[512,16]{0,1:T(8,128)}, u32[]{:S(2)}) copy-start(f32[512,16]{0,1:T(8,128)} %param.11) | copy-start | bytes 98308
  0.0 30.4 %collective-permute-start = (bf16[2,1,3072,1024]{3,2,1,0:T(8,128)(2,1)}, bf16[2,1,3072,1024]{3,2,1,0:T(8,128)(2,1)}, u32[]{:S(2)}, u32[]{:S(2)}) collective-permute-start(bf16[2,1,3072,1024]{3,2,1,0:T(8,128)(2,1)} %refs_1_.1), channel_id=1, source_target_pairs={{0,1},{1,0},{2,3},{3,2},{4,5},{5,4},{6,7},{7,6},{8,9},{9,8},{10,11... | collective-permute-start | bytes 37748744 | tf_op jit(solution)/shard_map/ppermute | solution.py:370

commit v5 on v4

--- a/solution.py
+++ b/solution.py
@@ -194,7 +194,7 @@
 
 STEP = 64
 SPAN = 256
-PIECES = 4
+PIECES = 2
 PITCH = 9
 DEPTH = 2
 
@@ -253,9 +253,11 @@
     groups = events // LANES
     count = length // SPAN
 
-    def save(k, s):
-        columns = pl.ds(pl.multiple_of(k * SPAN, LANES), SPAN)
-        return pltpu.make_async_copy(done.at[k, s], out_ref.at[s, :, columns], saved.at[k])
+    def save(k, s, at):
+        columns = pl.ds(pl.multiple_of(k * SPAN + at, LANES), LANES)
+        return pltpu.make_async_copy(
+            done.at[k, s, :, pl.ds(at, LANES)], out_ref.at[s, :, columns], saved.at[k, at // LANES]
+        )
 
     def gather(k, s, part, target):
         size = events // PIECES
@@ -298,6 +300,7 @@
                 done[k, s, g * LANES : (g + 1) * LANES, at : at + LANES] = jnp.transpose(
                     after[pl.ds(at * PITCH + s * groups + g, LANES, PITCH), :]
                 )
+            save(k, s, at).start()
 
     jobs = [(s, part) for s in range(stations) for part in range(PIECES)]
     steps = SPAN // STEP
@@ -310,8 +313,6 @@
             if (step + 1) * STEP % LANES == 0:
                 finish(k, ((step + 1) * STEP - LANES) // STEP)
         target[: taps * PITCH] = source[SPAN * PITCH : (SPAN + taps) * PITCH]
-        for s in range(stations):
-            save(k, s).start()
         return carry
 
     for s, part in jobs:
@@ -326,7 +327,8 @@
     lax.fori_loop(0, count // 2, pair, (silent,) * ((3**DEPTH - 1) // 2))
     for k in range(count):
         for s in range(stations):
-            save(k, s).wait()
+            for at in range(0, SPAN, LANES):
+                save(k, s, at).wait()
 
 
 def traces(chooser, scales, parts, taps, stations):
@@ -345,7 +347,7 @@
             pltpu.VMEM(((taps + SPAN + 1) * PITCH, LANES), jnp.float32),
             pltpu.VMEM(((SPAN + 1) * PITCH, LANES), jnp.float32),
             pltpu.VMEM((count, stations, events, SPAN), jnp.float32),
-            pltpu.SemaphoreType.DMA((count,)),
+            pltpu.SemaphoreType.DMA((count, SPAN // LANES)),
         ],
         compiler_params=pltpu.CompilerParams(vmem_limit_bytes=VMEM),
         name="trace_convolve",

time: 109 us -> 109 us (level)
  no operation moved by 1% of the time
where the time goes in v5:
time: 109 us
  blocking collectives  80.3 us (74%)
  Pallas kernels  28.2 us (26%)
    all_to_all x2, blocking collectives, exchange(): lax.all_to_all(value, 'blk', split_axis=0, concat_axis=0, tiled=True, axi...  80.3 us
    pallas_call x1, Pallas kernels, field(): pl.pallas_call(lambda *refs: field_kernel(capacity, tiles, *refs), in_spe...  16.6 us
    pallas_call x1, Pallas kernels, traces(): pl.pallas_call(lambda *refs: trace_kernel(taps, *refs), in_specs=[held, h...  7.81 us
    pallas_call x1, Pallas kernels, pack(): pl.pallas_call(lambda *refs: pack_kernel(capacity, *refs), grid=(blocks /...  3.78 us
  transfers between devices with their start and end apart: 1, of which 0 were waited for; matrix products, arithmetic and copies ran while one was open for 0% of the time, Pallas kernels for 3%

profile of v5, /device:TPU:0, one launch (start us, length us, event | category | flops | bytes accessed | tf_op | source)
XLA Modules:
  0.0 108.7 jit_solution(6214386177274308445)
XLA Ops:
  0.0 0.0 copy-start.1
  0.0 0.0 copy-start
  0.0 0.0 copy-start.2
  0.0 0.0 collective-permute-start
  0.0 3.8 %pack_rows.1 = bf16[32,136,128]{2,1,0:T(8,128)(2,1)} custom-call(s32[1,512]{1,0:T(1,128)} %bitcast.7, s32[1,512]{1,0:T(1,128)} %bitcast.9, bf16[512,512]{1,0:T(8,128)(2,1)} %refs_2_.1, bf16[512,512]{1,0:T(8,128)(2,1)} %refs_3_.1, bf16[6,512]{1,0:T(8,128)(2,1)} %bitcast.13), custom_call_target="tpu_custom_call" | custom-call | tf_op jit(solution)/shard_map/pack_rows/pallas_call | solution.py:58
  3.8 26.6 %all_to_all.10.refs_0_ = bf16[16,2,136,128]{3,2,1,0:T(8,128)(2,1)S(1)} all-to-all(bf16[16,2,136,128]{3,2,1,0:T(8,128)(2,1)} %bitcast.12), channel_id=1, replica_groups={{0,2,4,6,8,10,12,14,16,18,20,22,24,26,28,30},{1,3,5,7,9,11,13,15,17,19,..., dimensions={0} | all-to-all | bytes 2228224 | tf_op jit(solution)/shard_map/all_to_all | solution.py:368
  30.4 0.0 collective-permute-done.refs_2_
  30.4 0.0 copy-done.1
  30.4 0.0 copy-done
  30.4 0.0 copy-done.2
  30.4 16.6 %field_matmul.1 = (bf16[16,2,32,2048]{3,2,1,0:T(8,128)(2,1)S(1)}, bf16[512,1024]{1,0:T(8,128)(2,1)S(1)}, f32[36,8,128]{2,1,0:T(8,128)S(1)}) custom-call(bf16[16,2,136,128]{3,2,1,0:T(8,128)(2,1)S(1)} %all_to_all.10.refs_0_, bf16[2,1,3072,1024]{3,2,1,0:T(8,128)(2,1)} %refs_1_.1, bf16[2,1,3072,1024]{3,2,1,0:T(8,128)(2,1)} %collective-permute-done.refs_2_, ...), custom_call_target="tpu_custom_call" | custom-call | flops 12884901888 | bytes 25165824 | tf_op jit(solution)/shard_map/field_matmul/pallas_call | solution.py:168
  47.0 53.7 %all_to_all.11 = bf16[16,2,32,2048]{3,2,1,0:T(8,128)(2,1)S(1)} all-to-all(bf16[16,2,32,2048]{3,2,1,0:T(8,128)(2,1)S(1)} %get-tuple-element.10), channel_id=1, replica_groups={{0,2,4,6,8,10,12,14,16,18,20,22,24,26,28,30},{1,3,5,7,9,11,13,15,17,19,..., dimensions={0} | all-to-all | bytes 8388608 | tf_op jit(solution)/shard_map/all_to_all | solution.py:368
  100.7 7.8 %trace_convolve.1 = f32[2,512,1024]{2,1,0:T(8,128)} custom-call(bf16[512,1024]{1,0:T(8,128)(2,1)S(1)} %get-tuple-element.8.refs_0_, f32[36,8,128]{2,1,0:T(8,128)S(1)} %get-tuple-element.9.refs_1_, bf16[32,32,2048]{2,1,0:T(8,128)(2,1)S(1)} %bitcast.6), custom_call_target="tpu_custom_call" | custom-call | tf_op jit(solution)/shard_map/trace_convolve/pallas_call | solution.py:340
Async XLA Ops:
  0.0 30.4 %copy-start.1 = (s32[512]{0:T(512)S(1)}, s32[512]{0:T(512)}, u32[]{:S(2)}) copy-start(s32[512]{0:T(512)} %param.13) | copy-start | bytes 6148
  0.0 30.4 %copy-start = (s32[512]{0:T(512)S(1)}, s32[512]{0:T(512)}, u32[]{:S(2)}) copy-start(s32[512]{0:T(512)} %param.12) | copy-start | bytes 6148
  0.0 30.4 %copy-start.2 = (f32[512,16]{0,1:T(8,128)S(1)}, f32[512,16]{0,1:T(8,128)}, u32[]{:S(2)}) copy-start(f32[512,16]{0,1:T(8,128)} %param.11) | copy-start | bytes 98308
  0.0 30.4 %collective-permute-start = (bf16[2,1,3072,1024]{3,2,1,0:T(8,128)(2,1)}, bf16[2,1,3072,1024]{3,2,1,0:T(8,128)(2,1)}, u32[]{:S(2)}, u32[]{:S(2)}) collective-permute-start(bf16[2,1,3072,1024]{3,2,1,0:T(8,128)(2,1)} %refs_1_.1), channel_id=1, source_target_pairs={{0,1},{1,0},{2,3},{3,2},{4,5},{5,4},{6,7},{7,6},{8,9},{9,8},{10,11... | collective-permute-start | bytes 37748744 | tf_op jit(solution)/shard_map/ppermute | solution.py:372
